TPU v7x, 32 devices: a whole 2x2x4 slice. The times are simulated.
32 devices in a mesh: dp: 8 (over z, y), tensor: 4 (over x, core).
Axes of the slice: x: 2, y: 2, z: 4, core: 2. Of those that a mesh axis runs over, the one named last changes fastest.
Arguments:
- word_vectors: bfloat16 [16384, 768], P(('dp', 'tensor')), may hold values from -6 to 6
- position_table: bfloat16 [512, 768], P(('dp', 'tensor')), may hold values from -3 to 3
- horizontal_table: bfloat16 [1024, 768], P(('dp', 'tensor')), may hold values from -3 to 3
- vertical_table: bfloat16 [1024, 768], P(('dp', 'tensor')), may hold values from -3 to 3
- height_table: bfloat16 [1024, 768], P(('dp', 'tensor')), may hold values from -3 to 3
- width_table: bfloat16 [1024, 768], P(('dp', 'tensor')), may hold values from -3 to 3
- embed_gain: float32 [768], replicated, may hold values from 0.25 to 1.75
- embed_shift: float32 [768], replicated, may hold values from -3 to 3
- w_query: bfloat16 [768, 768], P('tensor'), may hold values from -0.21875 to 0.21875
- b_query: float32 [768], P('tensor'), may hold values from -3 to 3
- w_key: bfloat16 [768, 768], P('tensor'), may hold values from -0.21875 to 0.21875
- w_value: bfloat16 [768, 768], P('tensor'), may hold values from -0.21875 to 0.21875
- b_value: float32 [768], P('tensor'), may hold values from -3 to 3
- w_out: bfloat16 [768, 768], P('tensor'), may hold values from -1.25 to 1.25
- b_out: float32 [768], replicated, may hold values from -3 to 3
- attn_gain: float32 [768], replicated, may hold values from 0.25 to 1.75
- attn_shift: float32 [768], replicated, may hold values from -3 to 3
- w_in: bfloat16 [768, 3072], P(None, 'tensor'), may hold values from -0.21875 to 0.21875
- b_in: float32 [3072], P('tensor'), may hold values from -3 to 3
- w_down: bfloat16 [3072, 768], P('tensor'), may hold values from -0.109375 to 0.109375
- b_down: float32 [768], replicated, may hold values from -3 to 3
- ffn_gain: float32 [768], replicated, may hold values from 0.25 to 1.75
- ffn_shift: float32 [768], replicated, may hold values from -3 to 3
- boxes: int32 [4, 16384], P(None, ('dp', 'tensor')), may hold values from 0 to 1023
- segments: int32 [32, 512], P('dp'), may hold values from 0 to 7, never falling along the last dimension, each value on 1 to 128 neighbouring positions
- offsets: int32 [32, 8], P('dp'), may hold values from 0 to 384
- cotangent: float32 [16384, 768], P(('dp', 'tensor')), may hold values from -6 to 6
Outputs:
- layer_out: float32 [16384, 768], P(('dp', 'tensor'))
- grad_word: float32 [16384, 768], P(('dp', 'tensor'))
- grad_position_table: float32 [512, 768], P(('dp', 'tensor'))
- grad_horizontal_table: float32 [1024, 768], P(('dp', 'tensor'))
- grad_vertical_table: float32 [1024, 768], P(('dp', 'tensor'))
- grad_height_table: float32 [1024, 768], P(('dp', 'tensor'))
- grad_width_table: float32 [1024, 768], P(('dp', 'tensor'))
- grad_embed_gain: float32 [768], replicated
- grad_embed_shift: float32 [768], replicated
- grad_w_query: float32 [768, 768], P('tensor')
- grad_b_query: float32 [768], P('tensor')
- grad_w_key: float32 [768, 768], P('tensor')
- grad_w_value: float32 [768, 768], P('tensor')
- grad_b_value: float32 [768], P('tensor')
- grad_w_out: float32 [768, 768], P('tensor')
- grad_b_out: float32 [768], replicated
- grad_attn_gain: float32 [768], replicated
- grad_attn_shift: float32 [768], replicated
- grad_w_in: float32 [768, 3072], P(None, 'tensor')
- grad_b_in: float32 [3072], P('tensor')
- grad_w_down: float32 [3072, 768], P('tensor')
- grad_b_down: float32 [768], replicated
- grad_ffn_gain: float32 [768], replicated
- grad_ffn_shift: float32 [768], replicated
Inputs may be any that keep to these rules, and one draw needn't show every extreme that they name: `segments`: in each sequence page ids start at 0 and never fall; each of the 8 pages holds 1 to 128 tokens.
All inputs are finite; a program needn't handle non-finite values.
Results may differ from a plain program's by a relative error of at most 0.014.
Values may be sent and summed in bfloat16 or wider, within the bound.
A program may use at most 128 MiB of HBM per device.

v0:
```python
import jax
import jax.numpy as jnp
from jax import lax
from jax.sharding import PartitionSpec as P

HEAD = 64


epsilon = 1e-06
masked_score = -1e30


def product(left, right):
    return jnp.dot(left, right, preferred_element_type=jnp.float32)


def inner_rows(left, right):
    return lax.dot_general(
        left, right, (((0,), (0,)), ((), ())), preferred_element_type=jnp.float32
    )


def against_rows(left, right):
    return lax.dot_general(
        left, right, (((1,), (1,)), ((), ())), preferred_element_type=jnp.float32
    )


def page_positions(segments, offsets):
    length = segments.shape[1]
    places = jnp.arange(length, dtype=jnp.int32)
    labels = jnp.arange(offsets.shape[1], dtype=jnp.int32)
    member = segments[:, :, None] == labels[None, None, :]
    starts = jnp.min(jnp.where(member, places[None, :, None], length), axis=1)
    page_begin = jnp.sum(jnp.where(member, starts[:, None, :], 0), axis=2)
    page_shift = jnp.sum(jnp.where(member, offsets[:, None, :], 0), axis=2)
    return places[None, :] - page_begin + page_shift


def exact_gelu(values):
    return jax.nn.gelu(values, approximate=False)


def norm_forward(values, norm_gain, norm_shift):
    row_mean = jnp.mean(values, axis=1, keepdims=True)
    row_var = jnp.mean(values * values, axis=1, keepdims=True) - row_mean * row_mean
    scaled = lax.rsqrt(row_var + epsilon)
    centered = (values - row_mean) * scaled
    return (centered * norm_gain + norm_shift, centered, scaled)


def norm_backward(grad_out, centered, scaled, norm_gain):
    grad_centered = grad_out * norm_gain
    first_mean = jnp.mean(grad_centered, axis=1, keepdims=True)
    second_mean = jnp.mean(grad_centered * centered, axis=1, keepdims=True)
    grad_in = scaled * (grad_centered - first_mean - centered * second_mean)
    return (grad_in, jnp.sum(grad_out * centered, axis=0), jnp.sum(grad_out, axis=0))


def features(values):
    return lax.all_gather(values.astype(jnp.bfloat16), "tensor", axis=0, tiled=True)


def spread_sum(partial_term):
    return lax.psum_scatter(partial_term, "tensor", scatter_dimension=0, tiled=True)


def spread_grad(partial_term):
    return lax.psum_scatter(partial_term, "tensor", scatter_dimension=0, tiled=True)


def fold_back(grad_rows, weight, kept):
    shard_piece = lax.all_gather(grad_rows, "tensor", axis=0, tiled=True)
    grad_part = against_rows(shard_piece, weight)
    return (grad_part, inner_rows(kept, shard_piece))


def split_heads(values, sequences):
    return values.reshape(sequences, -1, values.shape[1] // HEAD, HEAD)


def page_scores(head_queries, head_keys, same_page):
    scores = jnp.einsum(
        "sqhd,skhd->shqk", head_queries, head_keys, preferred_element_type=jnp.float32
    ) * HEAD ** (-0.5)
    return jnp.where(same_page, scores, masked_score)


def body(
    word_vectors,
    position_table,
    horizontal_table,
    vertical_table,
    height_table,
    width_table,
    embed_gain,
    embed_shift,
    w_query,
    b_query,
    w_key,
    w_value,
    b_value,
    w_out,
    b_out,
    attn_gain,
    attn_shift,
    w_in,
    b_in,
    w_down,
    b_down,
    ffn_gain,
    ffn_shift,
    boxes,
    segments,
    offsets,
    cotangent,
):
    own_rows = word_vectors.shape[0]
    full_tables = (
        lax.all_gather(position_table, ("dp", "tensor"), axis=0, tiled=True),
        lax.all_gather(horizontal_table, ("dp", "tensor"), axis=0, tiled=True),
        lax.all_gather(vertical_table, ("dp", "tensor"), axis=0, tiled=True),
        lax.all_gather(height_table, ("dp", "tensor"), axis=0, tiled=True),
        lax.all_gather(width_table, ("dp", "tensor"), axis=0, tiled=True),
    )
    group_positions = page_positions(segments, offsets).reshape(-1)
    first_row = lax.axis_index("tensor") * own_rows
    positions = lax.dynamic_slice_in_dim(group_positions, first_row, own_rows, 0)
    left_edge = boxes[0]
    top_edge = boxes[1]
    right_edge = boxes[2]
    bottom_edge = boxes[3]
    box_height = jnp.abs(bottom_edge - top_edge)
    box_width = jnp.abs(right_edge - left_edge)
    lookups = (
        (full_tables[0], positions),
        (full_tables[1], left_edge),
        (full_tables[2], top_edge),
        (full_tables[1], right_edge),
        (full_tables[2], bottom_edge),
        (full_tables[3], box_height),
        (full_tables[4], box_width),
    )
    embedded = word_vectors.astype(jnp.float32)
    for lookup_table, row_index in lookups:
        embedded = embedded + jnp.take(lookup_table, row_index, axis=0).astype(jnp.float32)
    query_rows, key_rows, value_rows, out_rows, down_rows, in_rows = (
        w_query,
        w_key,
        w_value,
        w_out,
        w_down,
        w_in,
    )
    query_bias, value_bias, in_bias = (b_query, b_value, b_in)
    sequences = segments.shape[0]
    group_tokens = sequences * segments.shape[1]
    normed_in, centered_in, scaled_in = norm_forward(embedded, embed_gain, embed_shift)
    inputs_full = features(normed_in)
    queries = (against_rows(inputs_full, query_rows) + query_bias).astype(jnp.bfloat16)
    keys_all = against_rows(inputs_full, key_rows).astype(jnp.bfloat16)
    values_all = (against_rows(inputs_full, value_rows) + value_bias).astype(jnp.bfloat16)
    same_page = (segments[:, :, None] == segments[:, None, :])[:, None]
    head_queries = split_heads(queries, sequences)
    head_keys = split_heads(keys_all, sequences)
    head_values = split_heads(values_all, sequences)
    scores = page_scores(head_queries, head_keys, same_page)
    row_peak = jnp.max(scores, axis=-1, keepdims=True)
    exponent = jnp.exp(scores - row_peak)
    row_total = jnp.sum(exponent, axis=-1, keepdims=True)
    attention = (exponent / row_total).astype(jnp.bfloat16)
    log_total = row_peak + jnp.log(row_total)
    mixed_heads = jnp.einsum(
        "shqk,skhd->sqhd", attention, head_values, preferred_element_type=jnp.float32
    )
    mixed_low = mixed_heads.reshape(group_tokens, -1).astype(jnp.bfloat16)
    attn_term = product(mixed_low, out_rows)
    attn_total = spread_sum(attn_term)
    normed_mid, centered_mid, scaled_mid = norm_forward(
        attn_total + b_out + normed_in, attn_gain, attn_shift
    )
    mid_full = features(normed_mid)
    hidden_pre = product(mid_full, in_rows) + in_bias
    hidden_act, gelu_back = jax.vjp(exact_gelu, hidden_pre)
    hidden = hidden_act.astype(jnp.bfloat16)
    ffn_term = product(hidden, down_rows)
    ffn_total = spread_sum(ffn_term)
    layer_out, centered_out, scaled_out = norm_forward(
        ffn_total + b_down + normed_mid, ffn_gain, ffn_shift
    )
    grad_ffn_sum, grad_ffn_gain, grad_ffn_shift = norm_backward(
        cotangent, centered_out, scaled_out, ffn_gain
    )
    grad_b_down = jnp.sum(grad_ffn_sum, axis=0)
    ffn_low = grad_ffn_sum.astype(jnp.bfloat16)
    grad_hidden, grad_w_down = fold_back(ffn_low, down_rows, hidden)
    grad_pre = gelu_back(grad_hidden)[0].astype(jnp.bfloat16)
    grad_b_in = jnp.sum(grad_pre.astype(jnp.float32), axis=0)
    grad_w_in = inner_rows(mid_full, grad_pre)
    grad_mid = grad_ffn_sum + spread_grad(against_rows(grad_pre, in_rows))
    grad_attn_sum, grad_attn_gain, grad_attn_shift = norm_backward(
        grad_mid, centered_mid, scaled_mid, attn_gain
    )
    grad_b_out = jnp.sum(grad_attn_sum, axis=0)
    attn_low = grad_attn_sum.astype(jnp.bfloat16)
    grad_mixed, grad_w_out = fold_back(attn_low, out_rows, mixed_low)
    grad_heads = split_heads(grad_mixed.astype(jnp.bfloat16), sequences)
    again = jnp.exp(page_scores(head_queries, head_keys, same_page) - log_total)
    grad_attention = jnp.einsum(
        "sqhd,skhd->shqk", grad_heads, head_values, preferred_element_type=jnp.float32
    )
    grad_value_heads = jnp.einsum(
        "shqk,sqhd->skhd",
        again.astype(jnp.bfloat16),
        grad_heads,
        preferred_element_type=jnp.float32,
    )
    row_inner = jnp.sum(grad_attention * again, axis=-1, keepdims=True)
    grad_scores = (again * (grad_attention - row_inner)).astype(jnp.bfloat16)
    grad_query_heads = jnp.einsum(
        "shqk,skhd->sqhd", grad_scores, head_keys, preferred_element_type=jnp.float32
    ) * HEAD ** (-0.5)
    grad_key_heads = jnp.einsum(
        "shqk,sqhd->skhd", grad_scores, head_queries, preferred_element_type=jnp.float32
    ) * HEAD ** (-0.5)
    grad_queries = grad_query_heads.reshape(group_tokens, -1).astype(jnp.bfloat16)
    grad_keys = grad_key_heads.reshape(group_tokens, -1).astype(jnp.bfloat16)
    grad_values = grad_value_heads.reshape(group_tokens, -1).astype(jnp.bfloat16)
    grad_b_query = jnp.sum(grad_queries.astype(jnp.float32), axis=0)
    grad_b_value = jnp.sum(grad_values.astype(jnp.float32), axis=0)
    grad_w_query = inner_rows(grad_queries, inputs_full)
    grad_w_key = inner_rows(grad_keys, inputs_full)
    grad_w_value = inner_rows(grad_values, inputs_full)
    input_term = (
        product(grad_queries, query_rows)
        + product(grad_keys, key_rows)
        + product(grad_values, value_rows)
    )
    grad_in_sum = grad_attn_sum + spread_grad(input_term)
    grad_word, grad_embed_gain, grad_embed_shift = norm_backward(
        grad_in_sum, centered_in, scaled_in, embed_gain
    )
    position_rows = full_tables[0].shape[0]
    coord_rows = full_tables[1].shape[0]
    position_term = jax.ops.segment_sum(grad_word, positions, num_segments=position_rows)
    horizontal_term = jax.ops.segment_sum(
        grad_word, left_edge, num_segments=coord_rows
    ) + jax.ops.segment_sum(grad_word, right_edge, num_segments=coord_rows)
    vertical_term = jax.ops.segment_sum(
        grad_word, top_edge, num_segments=coord_rows
    ) + jax.ops.segment_sum(grad_word, bottom_edge, num_segments=coord_rows)
    height_term = jax.ops.segment_sum(grad_word, box_height, num_segments=coord_rows)
    width_term = jax.ops.segment_sum(grad_word, box_width, num_segments=coord_rows)
    table_sums = (
        lax.psum_scatter(position_term, ("dp", "tensor"), scatter_dimension=0, tiled=True),
        lax.psum_scatter(horizontal_term, ("dp", "tensor"), scatter_dimension=0, tiled=True),
        lax.psum_scatter(vertical_term, ("dp", "tensor"), scatter_dimension=0, tiled=True),
        lax.psum_scatter(height_term, ("dp", "tensor"), scatter_dimension=0, tiled=True),
        lax.psum_scatter(width_term, ("dp", "tensor"), scatter_dimension=0, tiled=True),
    )
    (
        grad_embed_gain,
        grad_embed_shift,
        grad_attn_gain,
        grad_attn_shift,
        grad_ffn_gain,
        grad_ffn_shift,
        grad_b_out,
        grad_b_down,
    ) = lax.psum(
        (
            grad_embed_gain,
            grad_embed_shift,
            grad_attn_gain,
            grad_attn_shift,
            grad_ffn_gain,
            grad_ffn_shift,
            grad_b_out,
            grad_b_down,
        ),
        ("dp", "tensor"),
    )
    (
        grad_w_query,
        grad_b_query,
        grad_w_key,
        grad_w_value,
        grad_b_value,
        grad_w_out,
        grad_w_in,
        grad_b_in,
        grad_w_down,
    ) = lax.psum(
        (
            grad_w_query,
            grad_b_query,
            grad_w_key,
            grad_w_value,
            grad_b_value,
            grad_w_out,
            grad_w_in,
            grad_b_in,
            grad_w_down,
        ),
        "dp",
    )
    return (
        layer_out,
        grad_word,
        table_sums[0],
        table_sums[1],
        table_sums[2],
        table_sums[3],
        table_sums[4],
        grad_embed_gain,
        grad_embed_shift,
        grad_w_query,
        grad_b_query,
        grad_w_key,
        grad_w_value,
        grad_b_value,
        grad_w_out,
        grad_b_out,
        grad_attn_gain,
        grad_attn_shift,
        grad_w_in,
        grad_b_in,
        grad_w_down,
        grad_b_down,
        grad_ffn_gain,
        grad_ffn_shift,
    )


def solution(mesh):
    return jax.shard_map(
        body,
        mesh=mesh,
        in_specs=(
            P(("dp", "tensor"), None),
            P(("dp", "tensor"), None),
            P(("dp", "tensor"), None),
            P(("dp", "tensor"), None),
            P(("dp", "tensor"), None),
            P(("dp", "tensor"), None),
            P(),
            P(),
            P("tensor", None),
            P("tensor"),
            P("tensor", None),
            P("tensor", None),
            P("tensor"),
            P("tensor", None),
            P(),
            P(),
            P(),
            P(None, "tensor"),
            P("tensor"),
            P("tensor", None),
            P(),
            P(),
            P(),
            P(None, ("dp", "tensor")),
            P("dp", None),
            P("dp", None),
            P(("dp", "tensor"), None),
        ),
        out_specs=(
            P(("dp", "tensor"), None),
            P(("dp", "tensor"), None),
            P(("dp", "tensor"), None),
            P(("dp", "tensor"), None),
            P(("dp", "tensor"), None),
            P(("dp", "tensor"), None),
            P(("dp", "tensor"), None),
            P(),
            P(),
            P("tensor", None),
            P("tensor"),
            P("tensor", None),
            P("tensor", None),
            P("tensor"),
            P("tensor", None),
            P(),
            P(),
            P(),
            P(None, "tensor"),
            P("tensor"),
            P("tensor", None),
            P(),
            P(),
            P(),
        ),
        check_vma=False,
    )
```

profile of v0, /device:TPU:0, one launch (start us, length us, event | category | flops | bytes accessed | tf_op | source)
XLA Modules:
  0.0 1530.5 jit_solution(12107149633034843603)
XLA Ops:
  12.9 45.7 %all_gather.27 = bf16[512,768]{1,0:T(8,128)(2,1)S(1)} all-gather(bf16[16,768]{1,0:T(8,128)(2,1)} %param.30), channel_id=1, replica_groups=mesh['dp'=8,'tensor'=4] {'dp','tensor'}, dimensions={0}, use_global_device_ids=true | all-gather | bytes 811008 | tf_op jit(solution)/shard_map/all_gather | solution.py:120
  63.1 6.6 all-gather.9.cloned.1.call-done
  69.7 4.9 gather_fusion.3
  77.4 49.0 %all-gather.11.cloned.1.call-done = bf16[1024,768]{1,0:T(8,128)(2,1)} async-done(((bf16[32,768]{1,0:T(8,128)(2,1)}), bf16[1024,768]{1,0:T(8,128)(2,1)}) %all-gather.11.cloned.1.call-update) | async-done | bytes 1572880 | tf_op jit(solution)/shard_map/all_gather | solution.py:122
  126.4 4.8 gather_fusion.4
  133.9 49.2 %all-gather.15.cloned.1.call-done = bf16[1024,768]{1,0:T(8,128)(2,1)} async-done(((bf16[32,768]{1,0:T(8,128)(2,1)}), bf16[1024,768]{1,0:T(8,128)(2,1)}) %all-gather.15.cloned.1.call-update) | async-done | bytes 1572880 | tf_op jit(solution)/shard_map/all_gather | solution.py:124
  183.1 4.7 gather_fusion.6
  187.8 51.9 %all-gather.13.cloned.1.call-done = bf16[1024,768]{1,0:T(8,128)(2,1)} async-done(((bf16[32,768]{1,0:T(8,128)(2,1)}), bf16[1024,768]{1,0:T(8,128)(2,1)}) %all-gather.13.cloned.1.call-update) | async-done | bytes 1572880 | tf_op jit(solution)/shard_map/all_gather | solution.py:123
  239.7 4.7 gather_fusion.5
  251.4 25.5 %all-gather.17.cloned.1.call-done = bf16[2048,768]{1,0:T(8,128)(2,1)} async-done(((bf16[512,768]{1,0:T(8,128)(2,1)}), bf16[2048,768]{1,0:T(8,128)(2,1)}) %all-gather.17.cloned.1.call-update) | async-done | bytes 3145744 | tf_op jit(solution)/shard_map/all_gather | solution.py:61
  281.4 4.0 fusion.13
  287.7 4.3 fusion.12
  295.0 4.3 fusion.51
  311.4 58.3 %reduce-scatter.10.cloned.1.call-done = f32[512,768]{1,0:T(8,128)} async-done(((f32[2048,768]{1,0:T(8,128)}), f32[512,768]{1,0:T(8,128)}) %reduce-scatter.10.cloned.1.call-update) | async-done | bytes 1572880 | tf_op jit(solution)/shard_map/reduce_scatter | solution.py:65
  374.8 28.6 %all-gather.19.cloned.1.call-done = bf16[2048,768]{1,0:T(8,128)(2,1)} async-done(((bf16[512,768]{1,0:T(8,128)(2,1)}), bf16[2048,768]{1,0:T(8,128)(2,1)}) %all-gather.19.cloned.1.call-update) | async-done | bytes 3145744 | tf_op jit(solution)/shard_map/all_gather | solution.py:61
  403.5 18.4 %multiply_convert_fusion.1 = (bf16[2048,768]{1,0:T(8,128)(2,1)S(1)}, f32[2048,768]{1,0:T(8,128)}, f32[2048,768]{1,0:T(8,128)}) fusion(f32[768]{0:T(1024)} %param.47, bf16[2048,768]{1,0:T(8,128)(2,1)} %all-gather.19.cloned.1.call-done, bf16[768,768]{1,0:T(8,128)(2,1)S(1)} %copy-done), kind=kOutput, calls=%fused_computation.29 | convolution fusion | flops 2519728128 | bytes 20057088 | tf_op jit(solution)/shard_map/dot_general | solution.py:14
  423.5 4.5 fusion.53
  428.1 58.5 %reduce-scatter.12.cloned.1.call-done = f32[512,768]{1,0:T(8,128)} async-done(((f32[2048,768]{1,0:T(8,128)}), f32[512,768]{1,0:T(8,128)}) %reduce-scatter.12.cloned.1.call-update) | async-done | bytes 1572880 | tf_op jit(solution)/shard_map/reduce_scatter | solution.py:65
  496.9 28.4 %all-gather.21.cloned.1.call-done = bf16[2048,768]{1,0:T(8,128)(2,1)} async-done(((bf16[512,768]{1,0:T(8,128)(2,1)}), bf16[2048,768]{1,0:T(8,128)(2,1)}) %all-gather.21.cloned.1.call-update) | async-done | bytes 3145744 | tf_op jit(solution)/shard_map/all_gather | solution.py:73
  525.3 11.0 convert_reduce_fusion
  538.1 4.5 fusion.54
  542.7 58.5 %reduce-scatter.14.cloned.1.call-done = f32[512,768]{1,0:T(8,128)} async-done(((f32[2048,768]{1,0:T(8,128)}), f32[512,768]{1,0:T(8,128)}) %reduce-scatter.14.cloned.1.call-update) | async-done | bytes 1572880 | tf_op jit(solution)/shard_map/reduce_scatter | solution.py:69
  601.1 3.8 multiply_reduce_fusion.2
  610.0 28.3 %all-gather.23.cloned.1.call-done = bf16[2048,768]{1,0:T(8,128)(2,1)} async-done(((bf16[512,768]{1,0:T(8,128)(2,1)}), bf16[2048,768]{1,0:T(8,128)(2,1)}) %all-gather.23.cloned.1.call-update) | async-done | bytes 3145744 | tf_op jit(solution)/shard_map/all_gather | solution.py:73
  638.3 3.9 convolution_convert_fusion
  644.6 6.9 convert_reduce_fusion.1
  651.5 8.9 multiply_reduce_fusion
  660.4 7.3 multiply_convert_fusion
  679.7 7.1 fusion.62
  686.8 4.2 fusion.61
  698.4 39.6 %reduce-scatter.16.cloned.1.call-done = f32[512,768]{1,0:T(8,128)} async-done(((f32[2048,768]{1,0:T(8,128)}), f32[512,768]{1,0:T(8,128)}) %reduce-scatter.16.cloned.1.call-update) | async-done | bytes 1572880 | tf_op jit(solution)/shard_map/reduce_scatter | solution.py:69
  742.4 6.3 scatter_custom_fusion
  748.7 7.0 scatter_custom_fusion.6
  755.8 6.5 scatter_custom_fusion.5
  762.4 6.7 scatter_custom_fusion.4
  769.1 6.5 scatter_custom_fusion.3
  775.6 5.0 add.270
  780.7 6.6 scatter_custom_fusion.2
  787.3 6.5 scatter_custom_fusion.1
  793.8 4.9 add.269
  799.3 23.9 %all-reduce.1 = (f32[192]{0:T(256)}, f32[192]{0:T(256)}, f32[768]{0:T(1024)}) all-reduce(f32[192]{0:T(256)S(1)} %reduce_sum.266, f32[192]{0:T(256)S(1)} %reduce_sum.268, f32[768]{0:T(1024)S(1)} %copy-done.53), channel_id=1, replica_groups=mesh['dp'=8,'tensor'=4] {'dp'}, use_global_device_ids=true, to_apply=%region_40.42 | all-reduce | flops 1152 | bytes 9216 | tf_op jit(solution)/shard_map/psum | solution.py:293
  823.3 39.4 %all-reduce = (f32[768]{0:T(1024)}, f32[768]{0:T(1024)}, f32[768]{0:T(1024)}, f32[768]{0:T(1024)}, f32[768]{0:T(1024)}, /*index=5*/f32[768]{0:T(1024)}, f32[768]{0:T(1024)}, f32[768]{0:T(1024)}) all-reduce(f32[768]{0:T(1024)S(1)} %get-tuple-element.29, ...), channel_id=1, replica_groups=mesh['dp'=8,'tensor'=4] {'dp','tensor'}, use_global_device_ids=true, to_apply=%region_35.37 | all-reduce | flops 6144 | bytes 49152 | tf_op jit(solution)/shard_map/psum | solution.py:270
  862.7 119.7 %all-reduce.5.cloned.1.call-done = (f32[192,768]{1,0:T(8,128)}, f32[192,768]{1,0:T(8,128)}, f32[192,768]{1,0:T(8,128)}, f32[192,768]{1,0:T(8,128)}, f32[768,768]{1,0:T(8,128)}, /*index=5*/f32[768,768]{1,0:T(8,128)}) async-done(((f32[192,768]{1,0:T(8,128)}, f32[192,768]{1,0:T(8,128)}, f32[192,768]{1,0:T(8,128)}, f32[192,768]{1,0:T(8,128)}, f32[768,768]{1,0:T(8,128)}, /*index=5*/f32[768,768]{1,0:T(8,128)}), ...) | async-done | bytes 7077904 | tf_op jit(solution)/shard_map/psum | solution.py:293
  982.5 102.5 %reduce-scatter.18.cloned.1.call-done = f32[16,768]{1,0:T(8,128)} async-done(((f32[512,768]{1,0:T(8,128)}), f32[16,768]{1,0:T(8,128)}) %reduce-scatter.18.cloned.1.call-update) | async-done | bytes 49168 | tf_op jit(solution)/shard_map/reduce_scatter | solution.py:255
  1084.9 107.3 %reduce-scatter.26.cloned.1.call-done = f32[32,768]{1,0:T(8,128)} async-done(((f32[1024,768]{1,0:T(8,128)}), f32[32,768]{1,0:T(8,128)}) %reduce-scatter.26.cloned.1.call-update) | async-done | bytes 98320 | tf_op jit(solution)/shard_map/reduce_scatter | solution.py:259
  1192.2 107.2 %reduce-scatter.24.cloned.1.call-done = f32[32,768]{1,0:T(8,128)} async-done(((f32[1024,768]{1,0:T(8,128)}), f32[32,768]{1,0:T(8,128)}) %reduce-scatter.24.cloned.1.call-update) | async-done | bytes 98320 | tf_op jit(solution)/shard_map/reduce_scatter | solution.py:258
  1299.5 107.3 %reduce-scatter.22.cloned.1.call-done = f32[32,768]{1,0:T(8,128)} async-done(((f32[1024,768]{1,0:T(8,128)}), f32[32,768]{1,0:T(8,128)}) %reduce-scatter.22.cloned.1.call-update) | async-done | bytes 98320 | tf_op jit(solution)/shard_map/reduce_scatter | solution.py:257
  1406.8 107.3 %reduce-scatter.20.cloned.1.call-done = f32[32,768]{1,0:T(8,128)} async-done(((f32[1024,768]{1,0:T(8,128)}), f32[32,768]{1,0:T(8,128)}) %reduce-scatter.20.cloned.1.call-update) | async-done | bytes 98320 | tf_op jit(solution)/shard_map/reduce_scatter | solution.py:256
  (243 shorter events, 104.2 us)
Async XLA Ops:
  7.2 396.3 %copy-start = (bf16[768,768]{1,0:T(8,128)(2,1)S(1)}, bf16[768,768]{1,0:T(8,128)(2,1)}, u32[]{:S(2)}) copy-start(bf16[768,768]{1,0:T(8,128)(2,1)} %param.46) | copy-start | bytes 3538948
  7.2 62.5 %all-gather.9.cloned.1.call-start = ((), (), s32[]{:S(2)}) async-start(), calls=%async_computation.9 | async-start | bytes 1622016 | tf_op jit(solution)/shard_map/all_gather | solution.py:121
  7.9 118.5 %all-gather.11.cloned.1.call-start = ((), (), s32[]{:S(2)}) async-start(), calls=%async_computation.10 | async-start | bytes 1622016 | tf_op jit(solution)/shard_map/all_gather | solution.py:122
  8.7 174.4 %all-gather.15.cloned.1.call-start = ((), (), s32[]{:S(2)}) async-start(), calls=%async_computation.12 | async-start | bytes 1622016 | tf_op jit(solution)/shard_map/all_gather | solution.py:124
  9.4 230.3 %all-gather.13.cloned.1.call-start = ((), (), s32[]{:S(2)}) async-start(), calls=%async_computation.11 | async-start | bytes 1622016 | tf_op jit(solution)/shard_map/all_gather | solution.py:123
  10.0 266.9 %all-gather.17.cloned.1.call-start = ((), (), s32[]{:S(2)}) async-start(), calls=%async_computation.13 | async-start | bytes 3932160 | tf_op jit(solution)/shard_map/all_gather | solution.py:61
  69.7 4.9 copy-start.3
  126.4 4.8 copy-start.4
  131.2 51.9 %copy-start.50 = (s32[1024]{0:T(1024)S(1)}, s32[1024]{0:T(1024)}, u32[]{:S(2)}) copy-start(s32[1024]{0:T(1024)} %pad_clamp_fusion) | copy-start | bytes 12292
  187.8 56.6 %copy-start.54 = (pred[512]{0:T(512)(128)(4,1)S(1)}, pred[512]{0:T(512)(128)(4,1)}, u32[]{:S(2)}) copy-start(pred[512]{0:T(512)(128)(4,1)} %get-tuple-element.75) | copy-start | bytes 1540
  249.3 120.3 %reduce-scatter.10.cloned.1.call-start = ((), (), s32[]{:S(2)}) async-start(), calls=%async_computation.14 | async-start | bytes 7864320 | tf_op jit(solution)/shard_map/reduce_scatter | solution.py:65
  251.4 30.0 %copy-start.57 = (f32[192]{0:T(256)S(1)}, f32[192]{0:T(256)}, u32[]{:S(2)}) copy-start(f32[192]{0:T(256)} %param.38) | copy-start | bytes 2308
  287.7 7.3 copy-start.14
  299.3 4.8 copy-start.2
  311.1 61.8 %copy-start.33 = (f32[768]{0:T(1024)S(1)}, f32[768]{0:T(1024)}, u32[]{:S(2)}) copy-start(f32[768]{0:T(1024)} %param.44) | copy-start | bytes 9220
  311.1 92.3 %all-gather.19.cloned.1.call-start = ((), (), s32[]{:S(2)}) async-start(), calls=%async_computation.15 | async-start | bytes 3932160 | tf_op jit(solution)/shard_map/all_gather | solution.py:61
  374.8 111.8 %reduce-scatter.12.cloned.1.call-start = ((), (), s32[]{:S(2)}) async-start(), calls=%async_computation.16 | async-start | bytes 7864320 | tf_op jit(solution)/shard_map/reduce_scatter | solution.py:65
  403.5 20.1 %copy-start.56 = (bf16[768,768]{1,0:T(8,128)(2,1)S(1)}, bf16[768,768]{1,0:T(8,128)(2,1)}, u32[]{:S(2)}) copy-start(bf16[768,768]{1,0:T(8,128)(2,1)} %param.48) | copy-start | bytes 3538948
  428.1 97.2 %all-gather.21.cloned.1.call-start = ((), (), s32[]{:S(2)}) async-start(), calls=%async_computation.17 | async-start | bytes 3932160 | tf_op jit(solution)/shard_map/all_gather | solution.py:73
  496.6 104.5 %reduce-scatter.14.cloned.1.call-start = ((), (), s32[]{:S(2)}) async-start(), calls=%async_computation.18 | async-start | bytes 7864320 | tf_op jit(solution)/shard_map/reduce_scatter | solution.py:69
  542.6 58.5 %copy-start.36 = (f32[512]{0:T(512)S(1)}, f32[512]{0:T(512)}, u32[]{:S(2)}) copy-start(f32[512]{0:T(512)} %copy-done.35) | copy-start | bytes 6148
  542.6 58.5 %copy-start.38 = (f32[512]{0:T(512)S(1)}, f32[512]{0:T(512)}, u32[]{:S(2)}) copy-start(f32[512]{0:T(512)} %copy-done.37) | copy-start | bytes 6148
  542.6 95.7 %all-gather.23.cloned.1.call-start = ((), (), s32[]{:S(2)}) async-start(), calls=%async_computation.19 | async-start | bytes 3932160 | tf_op jit(solution)/shard_map/all_gather | solution.py:73
  604.9 5.0 copy-start.29
  604.9 5.0 copy-start.31
  604.9 33.4 %copy-start.24 = (bf16[192,768]{1,0:T(8,128)(2,1)S(1)}, bf16[192,768]{1,0:T(8,128)(2,1)}, u32[]{:S(2)}) copy-start(bf16[192,768]{1,0:T(8,128)(2,1)} %param.42) | copy-start | bytes 884740
  609.6 128.4 %reduce-scatter.16.cloned.1.call-start = ((), (), s32[]{:S(2)}) async-start(), calls=%async_computation.20 | async-start | bytes 7864320 | tf_op jit(solution)/shard_map/reduce_scatter | solution.py:69
  644.5 7.0 copy-start.17
  644.6 15.8 %slice-start = ((s8[12582912]{0:T(1024)(128)(4,1)}), s8[4194304]{0:T(1024)(128)(4,1)S(1)}, s32[]{:S(2)}) async-start(s8[12582912]{0:T(1024)(128)(4,1)} %bitcast.81), calls=%async_computation.27 | async-start | bytes 8388608
  644.6 15.8 %slice-start.1 = ((s8[12582912]{0:T(1024)(128)(4,1)}), s8[4194304]{0:T(1024)(128)(4,1)S(1)}, s32[]{:S(2)}) async-start(s8[12582912]{0:T(1024)(128)(4,1)} %bitcast.81), calls=%async_computation.28 | async-start | bytes 8388608
  651.5 8.9 slice-start.2
  660.4 7.3 copy-start.15
  679.5 302.9 %all-reduce.5.cloned.1.call-start = ((), (), s32[]{:S(2)}) async-start(), calls=%async_computation.26 | async-start | bytes 14155776 | tf_op jit(solution)/shard_map/psum | solution.py:293
  679.7 7.1 copy-start.55
  679.7 7.1 copy-start.60
  698.3 386.6 %reduce-scatter.18.cloned.1.call-start = ((), (), s32[]{:S(2)}) async-start(), calls=%async_computation.21 | async-start | bytes 1622016 | tf_op jit(solution)/shard_map/reduce_scatter | solution.py:255
  748.7 443.5 %reduce-scatter.26.cloned.1.call-start = ((), (), s32[]{:S(2)}) async-start(), calls=%async_computation.25 | async-start | bytes 3244032 | tf_op jit(solution)/shard_map/reduce_scatter | solution.py:259
  755.8 543.7 %reduce-scatter.24.cloned.1.call-start = ((), (), s32[]{:S(2)}) async-start(), calls=%async_computation.24 | async-start | bytes 3244032 | tf_op jit(solution)/shard_map/reduce_scatter | solution.py:258
  762.4 644.4 %reduce-scatter.22.cloned.1.call-start = ((), (), s32[]{:S(2)}) async-start(), calls=%async_computation.23 | async-start | bytes 3244032 | tf_op jit(solution)/shard_map/reduce_scatter | solution.py:257
  780.7 733.4 %reduce-scatter.20.cloned.1.call-start = ((), (), s32[]{:S(2)}) async-start(), calls=%async_computation.22 | async-start | bytes 3244032 | tf_op jit(solution)/shard_map/reduce_scatter | solution.py:256
  798.6 24.6 %copy-start.43 = (f32[768]{0:T(1024)S(1)}, f32[768]{0:T(1024)}, u32[]{:S(2)}) copy-start(f32[768]{0:T(1024)} %get-tuple-element.25) | copy-start | bytes 9220
  798.6 24.6 %copy-start.44 = (f32[768]{0:T(1024)S(1)}, f32[768]{0:T(1024)}, u32[]{:S(2)}) copy-start(f32[768]{0:T(1024)} %get-tuple-element.34) | copy-start | bytes 9220
  798.6 24.6 %copy-start.45 = (f32[768]{0:T(1024)S(1)}, f32[768]{0:T(1024)}, u32[]{:S(2)}) copy-start(f32[768]{0:T(1024)} %get-tuple-element.66) | copy-start | bytes 9220
  798.7 24.6 %copy-start.47 = (f32[768]{0:T(1024)S(1)}, f32[768]{0:T(1024)}, u32[]{:S(2)}) copy-start(f32[768]{0:T(1024)} %get-tuple-element.64) | copy-start | bytes 9220
  798.7 24.6 %copy-start.48 = (f32[768]{0:T(1024)S(1)}, f32[768]{0:T(1024)}, u32[]{:S(2)}) copy-start(f32[768]{0:T(1024)} %get-tuple-element.27) | copy-start | bytes 9220
  798.7 24.6 %copy-start.49 = (f32[768]{0:T(1024)S(1)}, f32[768]{0:T(1024)}, u32[]{:S(2)}) copy-start(f32[768]{0:T(1024)} %get-tuple-element.35) | copy-start | bytes 9220
  982.4 537.3 %copy-start.22 = (f32[192,768]{1,0:T(8,128)S(1)}, f32[192,768]{1,0:T(8,128)}, u32[]{:S(2)}) copy-start(f32[192,768]{1,0:T(8,128)} %get-tuple-element.125) | copy-start | bytes 1769476
  982.5 538.2 %copy-start.21 = (f32[768,768]{1,0:T(8,128)S(1)}, f32[768,768]{1,0:T(8,128)}, u32[]{:S(2)}) copy-start(f32[768,768]{1,0:T(8,128)} %get-tuple-element.129) | copy-start | bytes 7077892
  (34 other events, 68.6 us)
Sparse Core Ops, SparseCore 0:
  10.9 58.7 all-gather.8
  72.6 53.7 all-gather.10
  129.3 53.8 all-gather.14
  185.9 53.8 all-gather.12
  249.4 27.4 all-gather.16
  311.2 58.3 reduce-scatter.9
  374.9 28.5 all-gather.18
  428.2 58.3 reduce-scatter.11
  496.8 28.5 all-gather.20
  542.7 58.3 reduce-scatter.13
  609.7 28.5 all-gather.22
  679.6 58.3 reduce-scatter.15
  744.2 238.1 all-reduce.4
  989.0 95.9 reduce-scatter.17
  1091.7 100.5 reduce-scatter.25
  1199.0 100.4 reduce-scatter.23
  1306.2 100.5 reduce-scatter.21
  1413.5 100.4 reduce-scatter.19
where the time goes:
time: 1540 us; the launch traced here: 1530 us
  waiting for transfers between devices  1140 us (74%)
  blocking collectives  109 us (7%)
  matrix products  107 us (7%)
  other arithmetic  101 us (7%)
  local copies, waits for them, and re-layouts  60.4 us (4%)
    psum x1, waiting for transfers between devices, body(): lax.psum((grad_w_query, grad_b_query, grad_w_key, grad_w_value, grad_b_va...  120 us
    reduce_scatter x2, waiting for transfers between devices, spread_sum(): lax.psum_scatter(partial_term, 'tensor', scatter_dimension=0, tiled=True)  117 us
    reduce_scatter x1, waiting for transfers between devices, body(): lax.psum_scatter(width_term, ('dp', 'tensor'), scatter_dimension=0, tiled...  107 us
    reduce_scatter x1, waiting for transfers between devices, body(): lax.psum_scatter(vertical_term, ('dp', 'tensor'), scatter_dimension=0, ti...  107 us
    reduce_scatter x1, waiting for transfers between devices, body(): lax.psum_scatter(horizontal_term, ('dp', 'tensor'), scatter_dimension=0,...  107 us
    reduce_scatter x1, waiting for transfers between devices, body(): lax.psum_scatter(height_term, ('dp', 'tensor'), scatter_dimension=0, tile...  107 us
    reduce_scatter x1, waiting for transfers between devices, body(): lax.psum_scatter(position_term, ('dp', 'tensor'), scatter_dimension=0, ti...  102 us
    reduce_scatter x2, waiting for transfers between devices, spread_grad(): lax.psum_scatter(partial_term, 'tensor', scatter_dimension=0, tiled=True)  98.1 us
  transfers between devices with their start and end apart: 18, of which 18 were waited for; matrix products, arithmetic and copies ran while one was open for 7% of the time, Pallas kernels for 0%

commit v1 on v0

v1 whole, which is shorter than its diff:
```python
import functools

import jax
import jax.numpy as jnp
from jax import lax
from jax.experimental import pallas as pl
from jax.experimental.pallas import tpu as pltpu
from jax.sharding import PartitionSpec as P

HEAD = 64
MESH = pl.DeviceIdType.MESH
BF16 = jnp.bfloat16
F32 = jnp.float32

epsilon = 1e-06
masked_score = -1e30


class Place:
    def __init__(self, bits):
        self.bits = bits
        self.dp = lax.axis_index("dp")
        self.t = lax.axis_index("tensor")
        self.core = self.t % 2
        self.half = self.t // 2

    def bit(self, i):
        return (self.dp // 2**i) % 2

    def dp_flip(self, mask):
        dp = self.dp
        for i in range(self.bits):
            if mask & (1 << i):
                dp = dp + 2**i - 2 * 2**i * self.bit(i)
        return dp

    def t_flip(self, mask):
        t = self.t
        if mask & 1:
            t = t + 1 - 2 * self.core
        if mask & 2:
            t = t + 2 - 4 * self.half
        return t

    def partner(self, way):
        if way == "core":
            return (self.dp, self.t_flip(1))
        if way == "half":
            return (self.dp, self.t_flip(2))
        return (self.dp_flip(1 << way), self.t)

    def greet(self):
        barrier = pltpu.get_barrier_semaphore()
        ways = ["core", "half"] + list(range(self.bits))
        for way in ways:
            pl.semaphore_signal(
                barrier, inc=1, device_id=self.partner(way), device_id_type=MESH
            )
        pl.semaphore_wait(barrier, len(ways))


class Links:
    def __init__(self, place, send_sems):
        self.place = place
        self.send_sems = send_sems
        self.sent = []
        self.count = 0

    def send(self, way, src, dst, recv_sem):
        copy = pltpu.make_async_remote_copy(
            src_ref=src,
            dst_ref=dst,
            send_sem=self.send_sems.at[self.count],
            recv_sem=recv_sem,
            device_id=self.place.partner(way),
            device_id_type=MESH,
        )
        copy.start()
        self.count += 1
        self.sent.append(copy)
        return copy

    def arrived(self, way, dst, recv_sem):
        pltpu.make_async_remote_copy(
            src_ref=dst,
            dst_ref=dst,
            send_sem=recv_sem,
            recv_sem=recv_sem,
            device_id=self.place.partner(way),
            device_id_type=MESH,
        ).wait_recv()

    def finish(self):
        for copy in self.sent:
            copy.wait_send()


def interleave(*steps):
    live = list(steps)
    while live:
        for step in list(live):
            try:
                next(step)
            except StopIteration:
                live.remove(step)


def tables_gather(place, links, own, full, sems):
    bits = place.bits
    line_masks = [2 * k for k in range(2 ** (bits - 1))]
    line_sem, half_sem, row_sem, cross_sem, core_sem = sems

    def at(dp_mask, t_mask):
        return full.at[place.dp_flip(dp_mask) * 4 + place.t_flip(t_mask)]

    def to_core(slab, key):
        links.send("core", slab, slab, core_sem.at[key])

    def onward(mask, slab_source, below):
        for b in range(below - 1, 0, -1):
            links.send(b, slab_source, at(mask, 0), line_sem.at[(mask | (1 << b)) // 2])
        links.send("half", slab_source, at(mask, 0), half_sem.at[mask // 2])
        links.send(0, slab_source, at(mask, 0), row_sem.at[mask // 2])
        links.send("core", slab_source, at(mask, 0), core_sem.at[mask * 2])

    onward(0, own, bits)
    yield
    order = []
    held = [0]
    for b in range(bits - 1, 0, -1):
        fresh = [m | (1 << b) for m in held]
        for m in fresh:
            order.append((m, b))
        held = held + fresh
    for mask, b in order:
        links.arrived(b, at(mask, 0), line_sem.at[mask // 2])
        onward(mask, at(mask, 0), b)
        yield
    low = place.bit(1)
    for pair in range(len(line_masks) // 2):
        base = 4 * pair
        for mask in (base, base + 2):
            links.arrived("half", at(mask, 2), half_sem.at[mask // 2])
            to_core(at(mask, 2), mask * 2 + 1)
            links.arrived(0, at(mask + 1, 0), row_sem.at[mask // 2])
            to_core(at(mask + 1, 0), (mask + 1) * 2)
        yield
        dp_other = place.dp_flip(base)
        clear = dp_other - 2 * low
        here_clear = clear * 4 + place.t_flip(2)
        links.send(0, full.at[here_clear], full.at[here_clear], cross_sem.at[2 * pair + low])
        row_dp = place.dp_flip(base + 1)
        raised = row_dp + 2 * (1 - low)
        here_raised = raised * 4 + place.t
        links.send(
            "half", full.at[here_raised], full.at[here_raised], cross_sem.at[2 * pair + 1 - low]
        )
        yield
    for pair in range(len(line_masks) // 2):
        base = 4 * pair
        dp_cross = place.dp_flip(base + 1)
        clear = (dp_cross - 2 * low) * 4 + place.t_flip(2)
        links.arrived(0, full.at[clear], cross_sem.at[2 * pair + low])
        links.send("core", full.at[clear], full.at[clear], core_sem.at[(base + 2 * low + 1) * 2 + 1])
        raised = (dp_cross + 2 * (1 - low)) * 4 + place.t_flip(2)
        links.arrived("half", full.at[raised], cross_sem.at[2 * pair + 1 - low])
        links.send(
            "core", full.at[raised], full.at[raised], core_sem.at[(base + 2 * (1 - low) + 1) * 2 + 1]
        )
        yield
    for mask in range(2**bits):
        for t_mask in (0, 2):
            links.arrived(
                "core", at(mask, t_mask + 1), core_sem.at[mask * 2 + t_mask // 2]
            )
    yield


def weight_gather(place, links, own, full, sems, local_sem):
    rows = own.shape[0] // 2
    near = pl.ds(pl.multiple_of(place.bit(0) * rows, rows), rows)
    far = pl.ds(pl.multiple_of((1 - place.bit(0)) * rows, rows), rows)
    other = place.t_flip(2)
    links.send("half", own.at[near], full.at[place.t, near], sems.at[0])
    links.send("core", own, full.at[place.t], sems.at[2])
    local = pltpu.make_async_copy(own, full.at[place.t], local_sem)
    local.start()
    yield
    links.arrived("half", full.at[other, near], sems.at[0])
    links.send(0, full.at[other, near], full.at[other, near], sems.at[1])
    links.send("core", full.at[other, near], full.at[other, near], sems.at[3])
    yield
    links.arrived(0, full.at[other, far], sems.at[1])
    links.send("core", full.at[other, far], full.at[other, far], sems.at[4])
    yield
    links.arrived("core", full.at[place.t_flip(1)], sems.at[2])
    links.arrived("core", full.at[place.t_flip(3), near], sems.at[3])
    links.arrived("core", full.at[place.t_flip(3), far], sems.at[4])
    local.wait()
    yield


def gather_kernel(
    bits,
    slab,
    square,
    wide,
    tall,
    tables,
    square_full,
    wide_full,
    tall_full,
    send_sems,
    line_sem,
    half_sem,
    row_sem,
    cross_sem,
    core_sem,
    weight_sems,
    local_sems,
):
    place = Place(bits)
    place.greet()
    links = Links(place, send_sems)
    local = pltpu.make_async_copy(
        slab, tables.at[place.dp * 4 + place.t], local_sems.at[3]
    )
    local.start()
    gathers = [
        weight_gather(place, links, own, full, weight_sems.at[i], local_sems.at[i])
        for i, (own, full) in enumerate(
            ((square, square_full), (wide, wide_full), (tall, tall_full))
        )
    ]
    interleave(
        tables_gather(
            place, links, slab, tables, (line_sem, half_sem, row_sem, cross_sem, core_sem)
        ),
        *gathers,
    )
    local.wait()
    links.finish()


def gather_all(devices, slab, square, wide, tall):
    bits = (devices // 4).bit_length() - 1
    lines = 2 ** (bits - 1)
    width = slab.shape[1]
    anywhere = pl.BlockSpec(memory_space=pl.ANY)
    full = jax.ShapeDtypeStruct((4,) + square.shape, BF16)
    return pl.pallas_call(
        functools.partial(gather_kernel, bits),
        out_shape=[jax.ShapeDtypeStruct((devices,) + slab.shape, BF16), full, full, full],
        in_specs=[anywhere] * 4,
        out_specs=[anywhere] * 4,
        scratch_shapes=[
            pltpu.SemaphoreType.DMA((10 * lines + 40 + lines * bits,)),
            pltpu.SemaphoreType.DMA((lines,)),
            pltpu.SemaphoreType.DMA((lines,)),
            pltpu.SemaphoreType.DMA((lines,)),
            pltpu.SemaphoreType.DMA((lines,)),
            pltpu.SemaphoreType.DMA((4 * lines,)),
            pltpu.SemaphoreType.DMA((3, 5)),
            pltpu.SemaphoreType.DMA((4,)),
        ],
        name="gather_all",
        compiler_params=pltpu.CompilerParams(collective_id=0, has_side_effects=True),
    )(slab, square, wide, tall)


def added(left, right):
    return (left.astype(F32) + right.astype(F32)).astype(BF16)


def ladder(rows, bits):
    left = [rows]
    for _ in range(bits):
        left.append(left[-1] // 2 if left[-1] % 32 == 0 else left[-1])
    return left


def weight_reduce(place, links, terms, total, from_core, from_half, from_dp, sems):
    t, other = place.t, place.t_flip(2)
    left = ladder(terms.shape[1], place.bits)
    links.send("core", terms.at[place.t_flip(3)], from_core.at[1], sems.at[1])
    links.send("core", terms.at[place.t_flip(1)], from_core.at[0], sems.at[0])
    yield
    links.arrived("core", from_core.at[1], sems.at[1])
    terms[other] = added(terms[other], from_core[1])
    links.send("half", terms.at[other], from_half, sems.at[2])
    yield
    links.arrived("core", from_core.at[0], sems.at[0])
    terms[t] = added(terms[t], from_core[0])
    yield
    links.arrived("half", from_half, sems.at[2])
    terms[t] = added(terms[t], from_half[...])
    start = 0
    starts = [0]
    used = 0
    for b in range(place.bits):
        rows = left[b + 1]
        halved = rows < left[b]
        mine = start + place.bit(b) * rows if halved else start
        theirs = start + (1 - place.bit(b)) * rows if halved else start
        mine = pl.ds(pl.multiple_of(mine, 16), rows)
        theirs = pl.ds(pl.multiple_of(theirs, 16), rows)
        landing = from_dp.at[pl.ds(used, rows)]
        copy = links.send(b, terms.at[t, theirs], landing, sems.at[3 + b])
        yield
        links.arrived(b, landing, sems.at[3 + b])
        if not halved:
            copy.wait_send()
            links.sent = [other for other in links.sent if other is not copy]
        terms[t, mine] = added(terms[t, mine], from_dp[pl.ds(used, rows)])
        used += rows
        if halved:
            start = start + place.bit(b) * rows
        starts.append(start)
    own = pl.ds(pl.multiple_of(start, 16), left[-1])
    total[own] = terms[t, own]
    for b in range(place.bits - 1, -1, -1):
        rows = left[b + 1]
        if rows == left[b]:
            continue
        mine = pl.ds(pl.multiple_of(starts[b] + place.bit(b) * rows, 16), rows)
        theirs = pl.ds(pl.multiple_of(starts[b] + (1 - place.bit(b)) * rows, 16), rows)
        links.send(b, total.at[mine], total.at[mine], sems.at[3 + place.bits + b])
        yield
        links.arrived(b, total.at[theirs], sems.at[3 + place.bits + b])
    yield


def table_reduce(place, links, terms, columns, order, halves, lines, half_sems, dp_sems):
    bits, core = place.bits, place.core

    def slab(mask, half):
        return terms.at[place.dp_flip(mask), half, core, :, columns]

    def add(mask, half, landed):
        dp = place.dp_flip(mask)
        terms[dp, half, core, :, columns] = added(
            terms[dp, half, core, :, columns], landed[...]
        )

    def lowest(mask):
        return (mask & -mask).bit_length() - 1 if mask else bits

    mine, theirs = place.half, 1 - place.half
    masks = sorted(range(2**bits), key=lambda m: (lowest(m), m))
    slot = 0
    base = {}
    for b in range(bits):
        for h in range(2 if (b == 0 and order == "row") else 1):
            base[b, h] = slot
            slot += 2 ** (bits - 1 - b)

    def index(b, h, mask):
        return base[b, h] + (mask >> (b + 1))

    def send_dp(b, mask, half, h):
        i = index(b, h, mask ^ (1 << b))
        links.send(b, slab(mask, half), lines.at[i], dp_sems.at[i])

    def take_dp(b, mask, half, h):
        i = index(b, h, mask)
        links.arrived(b, lines.at[i], dp_sems.at[i])
        add(mask, half, lines.at[i])

    if order == "half":
        for mask in masks:
            links.send("half", slab(mask, theirs), halves.at[mask], half_sems.at[mask])
        yield
        for mask in masks:
            links.arrived("half", halves.at[mask], half_sems.at[mask])
            add(mask, mine, halves.at[mask])
            if mask & 1:
                send_dp(0, mask, mine, 0)
            yield
    else:
        for h, half in ((1, theirs), (0, mine)):
            for mask in masks:
                if mask & 1:
                    send_dp(0, mask, half, h)
        yield
        kept = [m for m in masks if not m & 1]
        for mask in kept:
            take_dp(0, mask, theirs, 1)
            links.send("half", slab(mask, theirs), halves.at[mask], half_sems.at[mask])
            yield
        for mask in kept:
            take_dp(0, mask, mine, 0)
            yield
        for mask in kept:
            links.arrived("half", halves.at[mask], half_sems.at[mask])
            add(mask, mine, halves.at[mask])
            if bits > 1 and mask & 2:
                send_dp(1, mask, mine, 0)
            yield
    for b in range(0 if order == "half" else 1, bits):
        for mask in masks:
            if mask % (2 << b):
                continue
            take_dp(b, mask, mine, 0)
            if b + 1 < bits and mask & (2 << b):
                send_dp(b + 1, mask, mine, 0)
            yield


def vector_reduce(place, links, vectors, landing, sems):
    for i, way in enumerate(["core", "half"] + list(range(place.bits))):
        copy = links.send(way, vectors.at[i], landing.at[i], sems.at[i])
        yield
        links.arrived(way, landing.at[i], sems.at[i])
        vectors[i + 1] = vectors[i] + landing[i]


def reduce_kernel(
    bits,
    square,
    wide,
    tall,
    tables,
    vectors_in,
    square_sum,
    wide_sum,
    tall_sum,
    table_sum,
    vector_sum,
    from_core,
    from_half,
    from_dp,
    table_core,
    halves,
    lines_half,
    lines_row,
    vectors,
    vector_land,
    send_sems,
    weight_sems,
    core_sems,
    half_sems,
    line_half_sems,
    line_row_sems,
    vector_sems,
):
    place = Place(bits)
    place.greet()
    links = Links(place, send_sems)
    vectors[0] = vectors_in[...]
    split = tables.shape[-1] // 2

    def tables_all():
        theirs, mine = 1 - place.half, place.half
        for i, half in enumerate((theirs, mine)):
            links.send(
                "core",
                tables.at[:, half, 1 - place.core],
                table_core.at[i],
                core_sems.at[i],
            )
        yield
        for i, half in enumerate((theirs, mine)):
            links.arrived("core", table_core.at[i], core_sems.at[i])

            def add(d, carry):
                tables[d, half, place.core] = added(
                    tables[d, half, place.core], table_core[i, d]
                )
                return carry

            lax.fori_loop(0, 2**bits, add, 0)
        yield
        left = table_reduce(
            place,
            links,
            tables,
            pl.ds(0, split),
            "half",
            halves.at[0],
            lines_half,
            half_sems.at[0],
            line_half_sems,
        )
        right = table_reduce(
            place,
            links,
            tables,
            pl.ds(split, split),
            "row",
            halves.at[1],
            lines_row,
            half_sems.at[1],
            line_row_sems,
        )
        live = [left, right]
        while live:
            for step in list(live):
                try:
                    next(step)
                except StopIteration:
                    live.remove(step)
            yield
        table_sum[...] = tables[place.dp, place.half, place.core]

    steps = [
        weight_reduce(
            place,
            links,
            terms,
            total,
            from_core.at[i],
            from_half.at[i],
            from_dp.at[i],
            weight_sems.at[i],
        )
        for i, (terms, total) in enumerate(
            ((square, square_sum), (wide, wide_sum), (tall, tall_sum))
        )
    ]
    interleave(
        tables_all(), *steps, vector_reduce(place, links, vectors, vector_land, vector_sems)
    )
    links.finish()
    vector_sum[...] = vectors[bits + 2]


def reduce_all(devices, square, wide, tall, tables, vectors):
    bits = (devices // 4).bit_length() - 1
    dps = 2**bits
    rows, width = square.shape[1:]
    slab = tables.shape[3]
    landing = sum(ladder(rows, bits)[1:])
    in_vmem = pl.BlockSpec(memory_space=pltpu.VMEM)
    quarter = jax.ShapeDtypeStruct((rows, width), BF16)
    half_lines = dps - 1
    row_lines = dps - 1 + dps // 2
    return pl.pallas_call(
        functools.partial(reduce_kernel, bits),
        out_shape=[
            quarter,
            quarter,
            quarter,
            jax.ShapeDtypeStruct((slab, width), BF16),
            jax.ShapeDtypeStruct(vectors.shape, F32),
        ],
        in_specs=[in_vmem] * 5,
        out_specs=[in_vmem] * 5,
        scratch_shapes=[
            pltpu.VMEM((3, 2, rows, width), BF16),
            pltpu.VMEM((3, rows, width), BF16),
            pltpu.VMEM((3, landing, width), BF16),
            pltpu.VMEM((2, dps, slab, width), BF16),
            pltpu.VMEM((2, dps, slab, width // 2), BF16),
            pltpu.VMEM((half_lines, slab, width // 2), BF16),
            pltpu.VMEM((row_lines, slab, width // 2), BF16),
            pltpu.VMEM((bits + 3,) + vectors.shape, F32),
            pltpu.VMEM((bits + 2,) + vectors.shape, F32),
            pltpu.SemaphoreType.DMA((6 * dps + 60 + 8 * bits,)),
            pltpu.SemaphoreType.DMA((3, 3 + 2 * bits)),
            pltpu.SemaphoreType.DMA((2,)),
            pltpu.SemaphoreType.DMA((2, dps)),
            pltpu.SemaphoreType.DMA((half_lines,)),
            pltpu.SemaphoreType.DMA((row_lines,)),
            pltpu.SemaphoreType.DMA((bits + 2,)),
        ],
        name="reduce_all",
        compiler_params=pltpu.CompilerParams(
            collective_id=1, has_side_effects=True, vmem_limit_bytes=60 * 2**20
        ),
    )(square, wide, tall, tables, vectors)


def product(left, right):
    return jnp.dot(left, right, preferred_element_type=F32)


def inner_rows(left, right):
    return lax.dot_general(left, right, (((0,), (0,)), ((), ())), preferred_element_type=F32)


def against_rows(left, right):
    return lax.dot_general(left, right, (((1,), (1,)), ((), ())), preferred_element_type=F32)


def page_positions(segments, offsets):
    length = segments.shape[1]
    places = jnp.arange(length, dtype=jnp.int32)
    labels = jnp.arange(offsets.shape[1], dtype=jnp.int32)
    member = segments[:, :, None] == labels[None, None, :]
    starts = jnp.min(jnp.where(member, places[None, :, None], length), axis=1)
    page_begin = jnp.sum(jnp.where(member, starts[:, None, :], 0), axis=2)
    page_shift = jnp.sum(jnp.where(member, offsets[:, None, :], 0), axis=2)
    return places[None, :] - page_begin + page_shift


def exact_gelu(values):
    return jax.nn.gelu(values, approximate=False)


def norm_forward(values, norm_gain, norm_shift):
    row_mean = jnp.mean(values, axis=1, keepdims=True)
    row_var = jnp.mean(values * values, axis=1, keepdims=True) - row_mean * row_mean
    scaled = lax.rsqrt(row_var + epsilon)
    centered = (values - row_mean) * scaled
    return (centered * norm_gain + norm_shift, centered, scaled)


def norm_backward(grad_out, centered, scaled, norm_gain):
    grad_centered = grad_out * norm_gain
    first_mean = jnp.mean(grad_centered, axis=1, keepdims=True)
    second_mean = jnp.mean(grad_centered * centered, axis=1, keepdims=True)
    grad_in = scaled * (grad_centered - first_mean - centered * second_mean)
    return (grad_in, jnp.sum(grad_out * centered, axis=0), jnp.sum(grad_out, axis=0))


def split_heads(values):
    return values.reshape(values.shape[0], -1, HEAD)


def page_scores(head_queries, head_keys, same_page):
    scores = jnp.einsum(
        "qhd,khd->hqk", head_queries, head_keys, preferred_element_type=F32
    ) * HEAD ** (-0.5)
    return jnp.where(same_page, scores, masked_score)


def body(
    devices,
    word_vectors,
    position_table,
    horizontal_table,
    vertical_table,
    height_table,
    width_table,
    embed_gain,
    embed_shift,
    w_query,
    b_query,
    w_key,
    w_value,
    b_value,
    w_out,
    b_out,
    attn_gain,
    attn_shift,
    w_in,
    b_in,
    w_down,
    b_down,
    ffn_gain,
    ffn_shift,
    boxes,
    segments,
    offsets,
    cotangent,
):
    own_rows, width = word_vectors.shape
    t = lax.axis_index("tensor")
    owned = (position_table, horizontal_table, vertical_table, height_table, width_table)
    slab_rows = sum(table.shape[0] for table in owned)
    slab_padded = -(-slab_rows // 16) * 16
    slab = jnp.concatenate(owned, axis=0)
    slab = jnp.pad(slab, ((0, slab_padded - slab_rows), (0, 0)))
    square = jnp.concatenate((w_query, w_key, w_value, w_out), axis=0)
    tables, square_full, wide_full, tall_full = gather_all(
        devices, slab, square, w_in, w_down
    )
    tables = tables.reshape(devices * slab_padded, width)
    fourth = w_query.shape[0]
    query_rows, key_rows, value_rows, out_rows = (
        square_full[:, i * fourth : (i + 1) * fourth].reshape(width, width) for i in range(4)
    )
    in_rows = wide_full.transpose(1, 0, 2).reshape(width, -1)
    down_rows = tall_full.reshape(-1, width)
    query_bias, value_bias, in_bias = (
        lax.all_gather(bias, "tensor", axis=0, tiled=True) for bias in (b_query, b_value, b_in)
    )
    own_segments = lax.dynamic_slice_in_dim(segments, t, 1, 0)
    own_offsets = lax.dynamic_slice_in_dim(offsets, t, 1, 0)
    positions = page_positions(own_segments, own_offsets)[0]
    left_edge, top_edge, right_edge, bottom_edge = boxes
    lookups = (
        (0, positions),
        (1, left_edge),
        (2, top_edge),
        (1, right_edge),
        (2, bottom_edge),
        (3, jnp.abs(bottom_edge - top_edge)),
        (4, jnp.abs(right_edge - left_edge)),
    )
    first = [0]
    for table in owned:
        first.append(first[-1] + table.shape[0])
    counts = 0.0
    slots = jnp.arange(devices * slab_padded, dtype=jnp.int32)
    for k, rows in lookups:
        own = owned[k].shape[0]
        row_slots = rows // own * slab_padded + first[k] + rows % own
        counts = counts + (row_slots[:, None] == slots[None, :]).astype(F32)
    counts = counts.astype(BF16)
    embedded = word_vectors.astype(F32) + product(counts, tables)
    normed_in, centered_in, scaled_in = norm_forward(embedded, embed_gain, embed_shift)
    inputs_low = normed_in.astype(BF16)
    queries = (against_rows(inputs_low, query_rows) + query_bias).astype(BF16)
    keys_all = against_rows(inputs_low, key_rows).astype(BF16)
    values_all = (against_rows(inputs_low, value_rows) + value_bias).astype(BF16)
    same_page = own_segments[0][:, None] == own_segments[0][None, :]
    head_queries, head_keys, head_values = (
        split_heads(v) for v in (queries, keys_all, values_all)
    )
    scores = page_scores(head_queries, head_keys, same_page)
    row_peak = jnp.max(scores, axis=-1, keepdims=True)
    exponent = jnp.exp(scores - row_peak)
    row_total = jnp.sum(exponent, axis=-1, keepdims=True)
    again = exponent / row_total
    attention = again.astype(BF16)
    mixed_heads = jnp.einsum("hqk,khd->qhd", attention, head_values, preferred_element_type=F32)
    mixed_low = mixed_heads.reshape(own_rows, -1).astype(BF16)
    normed_mid, centered_mid, scaled_mid = norm_forward(
        product(mixed_low, out_rows) + b_out + normed_in, attn_gain, attn_shift
    )
    mid_low = normed_mid.astype(BF16)
    hidden_pre = product(mid_low, in_rows) + in_bias
    hidden_act, gelu_back = jax.vjp(exact_gelu, hidden_pre)
    hidden = hidden_act.astype(BF16)
    layer_out, centered_out, scaled_out = norm_forward(
        product(hidden, down_rows) + b_down + normed_mid, ffn_gain, ffn_shift
    )
    grad_ffn_sum, grad_ffn_gain, grad_ffn_shift = norm_backward(
        cotangent, centered_out, scaled_out, ffn_gain
    )
    grad_b_down = jnp.sum(grad_ffn_sum, axis=0)
    ffn_low = grad_ffn_sum.astype(BF16)
    grad_hidden = against_rows(ffn_low, down_rows)
    grad_w_down = inner_rows(hidden, ffn_low)
    grad_pre = gelu_back(grad_hidden)[0].astype(BF16)
    grad_b_in = jnp.sum(grad_pre.astype(F32), axis=0)
    grad_w_in = inner_rows(mid_low, grad_pre)
    grad_mid = grad_ffn_sum + against_rows(grad_pre, in_rows)
    grad_attn_sum, grad_attn_gain, grad_attn_shift = norm_backward(
        grad_mid, centered_mid, scaled_mid, attn_gain
    )
    grad_b_out = jnp.sum(grad_attn_sum, axis=0)
    attn_low = grad_attn_sum.astype(BF16)
    grad_mixed = against_rows(attn_low, out_rows)
    grad_w_out = inner_rows(mixed_low, attn_low)
    grad_heads = split_heads(grad_mixed.astype(BF16))
    grad_attention = jnp.einsum(
        "qhd,khd->hqk", grad_heads, head_values, preferred_element_type=F32
    )
    grad_values = jnp.einsum("hqk,qhd->khd", attention, grad_heads, preferred_element_type=F32)
    row_inner = jnp.sum(grad_attention * again, axis=-1, keepdims=True)
    grad_scores = (again * (grad_attention - row_inner)).astype(BF16)
    grad_queries = jnp.einsum(
        "hqk,khd->qhd", grad_scores, head_keys, preferred_element_type=F32
    ) * HEAD ** (-0.5)
    grad_keys = jnp.einsum(
        "hqk,qhd->khd", grad_scores, head_queries, preferred_element_type=F32
    ) * HEAD ** (-0.5)
    grad_queries, grad_keys, grad_values = (
        v.reshape(own_rows, -1).astype(BF16) for v in (grad_queries, grad_keys, grad_values)
    )
    grad_b_query = jnp.sum(grad_queries.astype(F32), axis=0)
    grad_b_value = jnp.sum(grad_values.astype(F32), axis=0)
    grad_square = jnp.stack(
        [
            v.reshape(4, fourth, width)
            for v in (
                inner_rows(grad_queries, inputs_low),
                inner_rows(grad_keys, inputs_low),
                inner_rows(grad_values, inputs_low),
                grad_w_out,
            )
        ],
        axis=1,
    ).reshape(4, width, width)
    grad_in_sum = (
        grad_attn_sum
        + product(grad_queries, query_rows)
        + product(grad_keys, key_rows)
        + product(grad_values, value_rows)
    )
    grad_word, grad_embed_gain, grad_embed_shift = norm_backward(
        grad_in_sum, centered_in, scaled_in, embed_gain
    )
    table_terms = inner_rows(counts, grad_word.astype(BF16)).astype(BF16)
    vectors = jnp.concatenate(
        [
            v.reshape(-1, width)
            for v in (
                grad_embed_gain,
                grad_embed_shift,
                grad_attn_gain,
                grad_attn_shift,
                grad_ffn_gain,
                grad_ffn_shift,
                grad_b_out,
                grad_b_down,
                grad_b_query,
                grad_b_value,
                grad_b_in,
            )
        ],
        axis=0,
    )
    vectors = jnp.pad(vectors, ((0, -vectors.shape[0] % 8), (0, 0)))
    square_sum, wide_sum, tall_sum, table_sum, vector_sum = reduce_all(
        devices,
        grad_square.astype(BF16),
        grad_w_in.reshape(width, 4, -1).transpose(1, 0, 2).astype(BF16),
        grad_w_down.reshape(4, -1, width).astype(BF16),
        table_terms.reshape(devices // 4, 2, 2, slab_padded, width),
        vectors,
    )
    square_sum = square_sum.astype(F32)
    table_sum = table_sum.astype(F32)
    bias_in = lax.dynamic_slice_in_dim(vector_sum[10:14].reshape(-1), t * b_in.shape[0], b_in.shape[0])
    bias_query, bias_value = (
        lax.dynamic_slice_in_dim(vector_sum[i], t * fourth, fourth) for i in (8, 9)
    )
    return (
        layer_out,
        grad_word,
        *(table_sum[first[k] : first[k + 1]] for k in range(5)),
        vector_sum[0],
        vector_sum[1],
        square_sum[:fourth],
        bias_query,
        square_sum[fourth : 2 * fourth],
        square_sum[2 * fourth : 3 * fourth],
        bias_value,
        square_sum[3 * fourth :],
        vector_sum[6],
        vector_sum[2],
        vector_sum[3],
        wide_sum.astype(F32),
        bias_in,
        tall_sum.astype(F32),
        vector_sum[7],
        vector_sum[4],
        vector_sum[5],
    )


def solution(mesh):
    devices = mesh.shape["dp"] * mesh.shape["tensor"]
    both = P(("dp", "tensor"), None)
    rows = P("tensor", None)
    return jax.shard_map(
        functools.partial(body, devices),
        mesh=mesh,
        in_specs=(
            *(both,) * 6,
            P(),
            P(),
            rows,
            P("tensor"),
            rows,
            rows,
            P("tensor"),
            rows,
            P(),
            P(),
            P(),
            P(None, "tensor"),
            P("tensor"),
            rows,
            P(),
            P(),
            P(),
            P(None, ("dp", "tensor")),
            P("dp", None),
            P("dp", None),
            both,
        ),
        out_specs=(
            *(both,) * 7,
            P(),
            P(),
            rows,
            P("tensor"),
            rows,
            rows,
            P("tensor"),
            rows,
            P(),
            P(),
            P(),
            P(None, "tensor"),
            P("tensor"),
            rows,
            P(),
            P(),
            P(),
        ),
        check_vma=False,
    )
```

time: 1540 us -> 620 us (0.40)
  waiting for transfers between devices: 1140 us -> 0 us
  Pallas kernels: 0 us -> 371 us
  blocking collectives: 109 us -> 14.2 us
  other arithmetic: 101 us -> 21.4 us
  matrix products: 107 us -> 140 us
    reduce_scatter x9 -> x0, waiting for transfers between devices: 746 us -> none  [the longest x2 117 us: spread_sum(): lax.psum_scatter(partial_term, 'tensor', scatter_dimension=0, tiled=True)]
    pallas_call x0 -> x2, Pallas kernels: none -> 371 us  [the longest x1 239 us: reduce_all(): pl.pallas_call(functools.partial(reduce_kernel, bits), out_shape=[quarter...]
    all_gather x8 -> x0, waiting for transfers between devices: 268 us -> none  [the longest x2 56.8 us: fold_back(): shard_piece = lax.all_gather(grad_rows, 'tensor', axis=0, tiled=True)]
    psum x1 -> x0, waiting for transfers between devices: 120 us -> none  [body(): lax.psum((grad_w_query, grad_b_query, grad_w_key, grad_w_value, grad_b_va...]
    psum x2 -> x0, blocking collectives: 63.3 us -> none  [the longest x1 39.4 us: body(): lax.psum((grad_embed_gain, grad_embed_shift, grad_attn_gain, grad_attn_sh...]
    scatter-add x7 -> x0, other arithmetic: 46.1 us -> none  [the longest x1 7 us: body(): jax.ops.segment_sum(grad_word, box_width, num_segments=coord_rows)]
    all_gather x1, blocking collectives: 45.7 us -> 5.18 us  [body(): lax.all_gather(bias, 'tensor', axis=0, tiled=True)]
    gather x7 -> x0, local copies, waits for them, and re-layouts: 26.6 us -> none  [body(): jnp.take(lookup_table, row_index, axis=0).astype(jnp.float32)]
  transfers between devices with their start and end apart: 18 -> 0, of which waited for: 18 -> 0; matrix products, arithmetic and copies ran while one was open for 7% -> 0% of each run, Pallas kernels for 0% -> 0%
where the time goes in v1:
time: 620 us; the launch traced here: 609 us
  Pallas kernels  371 us (60%)
  matrix products  140 us (23%)
  local copies, waits for them, and re-layouts  60.3 us (10%)
  other arithmetic  21.4 us (3%)
  blocking collectives  14.2 us (2%)
    pallas_call x1, Pallas kernels, reduce_all(): pl.pallas_call(functools.partial(reduce_kernel, bits), out_shape=[quarter...  239 us
    pallas_call x1, Pallas kernels, gather_all(): pl.pallas_call(functools.partial(gather_kernel, bits), out_shape=[jax.Sha...  133 us
    dot_general x7, matrix products, product(): return jnp.dot(left, right, preferred_element_type=F32)  44 us
    dot_general x7, matrix products, inner_rows(): lax.dot_general(left, right, (((0,), (0,)), ((), ())), preferred_element_...  34.2 us
    dot_general x6, matrix products, against_rows(): lax.dot_general(left, right, (((1,), (1,)), ((), ())), preferred_element_...  25.2 us
    convert_element_type x2, local copies, waits for them, and re-layouts, body(): grad_w_in.reshape(width, 4, -1).transpose(1, 0, 2).astype(BF16)  13.7 us

profile of v1, /device:TPU:0, one launch (start us, length us, event | category | flops | bytes accessed | tf_op | source)
XLA Modules:
  0.0 609.4 jit_solution(3891725599106912608)
XLA Ops:
  5.9 9.0 %all-reduce.3 = (f32[768]{0:T(1024)}, f32[768]{0:T(1024)}) all-reduce(f32[768]{0:T(1024)S(1)} %dynamic-update-slice, f32[768]{0:T(1024)S(1)} %dynamic-update-slice.1), channel_id=1, replica_groups=mesh['dp'=8,'tensor'=4] {'tensor'}, use_global_device_ids=true, to_apply=%add.1 | all-reduce | flops 1536 | bytes 12288
  16.0 5.2 all-gather
  26.0 2.3 pad_maximum_fusion.1.square
  28.3 132.8 %gather_all.1 = (bf16[32,144,768]{2,1,0:T(8,128)(2,1)}, bf16[4,768,768]{2,1,0:T(8,128)(2,1)}, bf16[4,768,768]{2,1,0:T(8,128)(2,1)}, bf16[4,768,768]{2,1,0:T(8,128)(2,1)}) custom-call(bf16[144,768]{1,0:T(8,128)(2,1)} %copy-done.31, bf16[768,768]{1,0:T(8,128)(2,1)} %pad_maximum_fusion.1.square, bf16[768,768]{1,0:T(8,128)(2,1)} %wide.1, bf16[768,768]{1,0:T(8,128)(2,1)} %tall.1), custom_call_target="tpu_custom_call" | custom-call | tf_op jit(solution)/shard_map/gather_all/pallas_call | solution.py:251
  161.3 14.9 %fusion.84 = (f32[512]{0:T(512)S(1)}, f32[512]{0:T(512)S(1)}, f32[512,768]{1,0:T(8,128)S(1)}) fusion(bf16[4608,768]{1,0:T(8,128)(2,1)} %bitcast.163, s32[512]{0:T(512)S(1)} %get-tuple-element.112, s32[512]{0:T(512)S(1)} %get-tuple-element.115, s32[512]{0:T(512)S(1)} %get-tuple-element.116, s32[512]{0:T(512)S(1)} %get-tuple-element.113, ...), kind=kOutput, calls=%fused_computation.222 | convolution fusion | flops 3675388928 | bytes 9455616 | tf_op jit(solution)/shard_map/dot_general | solution.py:574
  176.5 7.0 %copy.92 = bf16[768,4,768]{0,2,1:T(8,128)(2,1)} copy(bf16[768,4,768]{2,0,1:T(8,128)(2,1)} %bitcast.130) | data formatting | bytes 9437184 | tf_op jit(solution)/shard_map/transpose | solution.py:673
  183.4 4.1 fusion.88
  188.6 1.7 add_convert_fusion.4
  190.3 1.4 copy.89
  191.7 3.1 add_convert_fusion.5
  194.8 2.3 copy.88
  197.1 3.2 convolution_convert_fusion.8
  200.4 1.4 copy.90
  201.8 7.6 %fusion.93 = (f32[12,512]{1,0:T(8,128)S(1)}, f32[12,512,512]{1,2,0:T(8,128)}) fusion(pred[512,512]{0,1:T(8,128)(4,1)S(1)} %copy-done.32, bf16[512,12,64]{0,2,1:T(8,128)(2,1)S(1)} %bitcast.132, bf16[512,12,64]{0,2,1:T(8,128)(2,1)S(1)} %bitcast.122), kind=kOutput, calls=%fused_computation.230 | convolution fusion | flops 415236608 | bytes 14442496 | tf_op jit(solution)/shard_map/sub | solution.py:713
  209.4 6.1 %fusion.20 = bf16[12,64,512]{2,1,0:T(8,128)(2,1)S(1)} fusion(bf16[512,12,64]{0,2,1:T(8,128)(2,1)} %bitcast.146, f32[12,512,512]{1,2,0:T(8,128)} %get-tuple-element.119, f32[12,512]{1,0:T(8,128)S(1)} %get-tuple-element.118), kind=kOutput, calls=%fused_computation.84 | convolution fusion | flops 409337856 | bytes 14180352 | tf_op jit(solution)/shard_map/hqk,khd->qhd/dot_general | solution.py:717
  215.7 1.3 fusion.83
  217.0 20.2 %multiply_convert_fusion.1 = (bf16[512,3072]{1,0:T(8,128)(2,1)S(1)}, f32[512,3072]{1,0:T(8,128)}, f32[512,3072]{1,0:T(8,128)}) fusion(f32[3072]{0:T(1024)S(1)} %bitcast.155, bf16[768,3072]{0,1:T(8,128)(2,1)} %bitcast.126, f32[512,768]{1,0:T(8,128)S(1)} %get-tuple-element.120, f32[768]{0:T(1024)S(1)} %copy-done.58, f32[768]{0:T(1024)S(1)} %copy-done.39, ...), kind=kOutput, calls=%fused_computation.19 | convolution fusion | flops 2521694208 | bytes 22042624 | tf_op jit(solution)/shard_map/dot_general | solution.py:574
  237.3 2.9 fusion.82
  241.2 1.8 fusion.85
  242.9 9.4 %convert_reduce_fusion = (f32[3072]{0:T(1024)S(1)}, bf16[512,3072]{1,0:T(8,128)(2,1)}) fusion(f32[512,3072]{1,0:T(8,128)} %get-tuple-element.77, bf16[3072,768]{1,0:T(8,128)(2,1)S(1)} %bitcast.167, f32[512,768]{1,0:T(8,128)S(1)} %get-tuple-element.73, f32[512,3072]{1,0:T(8,128)} %get-tuple-element.121, f32[3072]{0:T(1024)S(1)} %bitcast.156), kind=kOutput, calls=%fused_computation.17 | convolution fusion | flops 2443047936 | bytes 22044672 | tf_op jit(solution)/shard_map/dot_general | solution.py:582
  252.3 6.0 multiply_reduce_fusion.2
  258.4 2.5 fusion.86
  261.7 4.8 convolution_convert_fusion.2
  266.5 1.7 convolution_convert_fusion.7
  268.2 2.3 copy.93
  270.5 6.7 %copy.98 = bf16[768,3072]{0,1:T(8,128)(2,1)} copy(bf16[768,3072]{1,0:T(8,128)(2,1)} %convolution_convert_fusion.2) | data formatting | bytes 9437184 | tf_op jit(solution)/shard_map/convert_element_type | solution.py:810
  277.2 7.0 %copy.99 = bf16[768,4,768]{2,0,1:T(8,128)(2,1)} copy(bf16[768,4,768]{0,2,1:T(8,128)(2,1)} %bitcast.116) | data formatting | bytes 9437184 | tf_op jit(solution)/shard_map/convert_element_type | solution.py:810
  284.3 3.0 fusion.19
  287.3 7.5 %convert_reduce_fusion.1 = (f32[12,64]{1,0:T(8,128)S(1)}, bf16[12,64,512]{2,1,0:T(8,128)(2,1)}) fusion(bf16[512,12,64]{0,2,1:T(8,128)(2,1)S(1)} %bitcast.148, f32[12,512,512]{1,2,0:T(8,128)} %get-tuple-element.119, f32[12,512]{1,0:T(8,128)S(1)} %copy-done.35), kind=kOutput, calls=%fused_computation.45 | convolution fusion | flops 410123520 | bytes 14183424 | tf_op jit(solution)/shard_map/hqk,qhd->khd/dot_general | solution.py:751
  294.8 3.4 fusion.18
  298.2 6.8 %convolution_convert_fusion.1 = bf16[3072,768]{1,0:T(8,128)(2,1)} fusion(bf16[512,3072]{1,0:T(8,128)(2,1)} %copy-done.60, f32[512,768]{1,0:T(8,128)S(1)} %copy-done.16), kind=kOutput, calls=%fused_computation.37 | convolution fusion | flops 2418671616 | bytes 9437184 | tf_op jit(solution)/shard_map/dot_general | solution.py:578
  305.0 10.2 %multiply_reduce_fusion = (f32[12,512]{1,0:T(8,128)S(1)}, f32[12,512,512]{1,2,0:T(8,128)}) fusion(f32[12,512,512]{1,2,0:T(8,128)} %get-tuple-element.119, f32[12,512]{1,0:T(8,128)S(1)} %copy-done.35, bf16[512,12,64]{0,2,1:T(8,128)(2,1)S(1)} %bitcast.149, bf16[512,12,64]{0,2,1:T(8,128)(2,1)S(1)} %bitcast.147), kind=kOutput, calls=%fused_computation.2 | convolution fusion | flops 412084224 | bytes 26787840 | tf_op jit(solution)/shard_map/qhd,khd->hqk/dot_general | solution.py:748
  317.7 6.8 %multiply_convert_fusion = bf16[12,512,512]{1,2,0:T(8,128)(2,1)S(1)} fusion(f32[12,512,512]{1,2,0:T(8,128)} %get-tuple-element.125, f32[12,512]{1,0:T(8,128)S(1)} %get-tuple-element.124, f32[12,512,512]{1,2,0:T(8,128)S(1)} %bitcast.120, f32[12,512]{1,0:T(8,128)S(1)} %copy-done.35), kind=kLoop, calls=%fused_computation.1 | loop fusion | flops 12582912 | bytes 31506432 | tf_op jit(solution)/shard_map/convert_element_type | solution.py:753
  324.5 2.9 multiply_convert_fusion.2
  327.4 2.0 convert_reduce_fusion.2
  329.5 2.5 fusion.95
  333.4 1.5 multiply_reduce_fusion.3
  335.0 1.6 subtract_multiply_fusion
  337.3 2.1 fusion.17
  341.1 2.6 copy.97
  343.8 13.4 %convolution_convert_fusion = bf16[4608,768]{1,0:T(8,128)(2,1)} fusion(s32[512]{0:T(512)S(1)} %copy-done.50, s32[512]{0:T(512)S(1)} %copy-done.44, s32[512]{0:T(512)S(1)} %copy-done.46, s32[512]{0:T(512)S(1)} %copy-done.52, s32[512]{0:T(512)S(1)} %copy-done.42, s32[512]{0:T(512)S(1)} %copy-done.48, s32[512]{0:T(512)S(1)} %copy-done.54, ...), kind=kOutput, calls=%fused_computation.15 | convolution fusion | flops 3677356032 | bytes 8665088 | tf_op jit(solution)/shard_map/dot_general | solution.py:578
  357.2 238.6 %reduce_all.1 = (bf16[768,768]{1,0:T(8,128)(2,1)}, bf16[768,768]{1,0:T(8,128)(2,1)}, bf16[768,768]{1,0:T(8,128)(2,1)}, bf16[144,768]{1,0:T(8,128)(2,1)}, f32[16,768]{1,0:T(8,128)}) custom-call(bf16[4,768,768]{2,1,0:T(8,128)(2,1)} %bitcast.118, bf16[4,768,768]{2,1,0:T(8,128)(2,1)} %bitcast.117, bf16[4,768,768]{2,1,0:T(8,128)(2,1)} %bitcast.131, ...), custom_call_target="tpu_custom_call" | custom-call | tf_op jit(solution)/shard_map/reduce_all/pallas_call | solution.py:537
  596.6 1.7 fusion.91
  600.3 1.4 slice.96
  601.7 1.6 fusion.90
  603.3 2.8 fusion.89
  606.0 1.6 convert_element_type.201
  607.6 1.6 convert_element_type.202
  (192 shorter events, 22.7 us)
Async XLA Ops:
  15.9 145.3 %copy-start.47 = (s32[512]{0:T(512)}, s32[512]{0:T(512)S(1)}, u32[]{:S(2)}) copy-start(s32[512]{0:T(512)S(1)} %get-tuple-element.111) | copy-start | bytes 6148
  15.9 145.3 %copy-start.49 = (s32[512]{0:T(512)}, s32[512]{0:T(512)S(1)}, u32[]{:S(2)}) copy-start(s32[512]{0:T(512)S(1)} %get-tuple-element.112) | copy-start | bytes 6148
  15.9 145.3 %copy-start.51 = (s32[512]{0:T(512)}, s32[512]{0:T(512)S(1)}, u32[]{:S(2)}) copy-start(s32[512]{0:T(512)S(1)} %get-tuple-element.113) | copy-start | bytes 6148
  15.9 145.3 %copy-start.53 = (s32[512]{0:T(512)}, s32[512]{0:T(512)S(1)}, u32[]{:S(2)}) copy-start(s32[512]{0:T(512)S(1)} %get-tuple-element.133) | copy-start | bytes 6148
  15.9 145.3 %copy-start.41 = (s32[512]{0:T(512)}, s32[512]{0:T(512)S(1)}, u32[]{:S(2)}) copy-start(s32[512]{0:T(512)S(1)} %get-tuple-element.114) | copy-start | bytes 6148
  15.9 145.3 %copy-start.43 = (s32[512]{0:T(512)}, s32[512]{0:T(512)S(1)}, u32[]{:S(2)}) copy-start(s32[512]{0:T(512)S(1)} %get-tuple-element.115) | copy-start | bytes 6148
  16.0 145.3 %copy-start.45 = (s32[512]{0:T(512)}, s32[512]{0:T(512)S(1)}, u32[]{:S(2)}) copy-start(s32[512]{0:T(512)S(1)} %get-tuple-element.116) | copy-start | bytes 6148
  25.1 3.2 copy-start.31
  25.1 136.1 %copy-start.55 = (bf16[512,768]{1,0:T(8,128)(2,1)S(1)}, bf16[512,768]{1,0:T(8,128)(2,1)}, u32[]{:S(2)}) copy-start(bf16[512,768]{1,0:T(8,128)(2,1)} %param.27) | copy-start | bytes 2359300
  161.2 14.9 %copy-start.33 = (f32[768]{0:T(1024)S(1)}, f32[768]{0:T(1024)}, u32[]{:S(2)}) copy-start(f32[768]{0:T(1024)} %param.33) | copy-start | bytes 9220
  161.2 14.9 %copy-start.38 = (f32[768]{0:T(1024)S(1)}, f32[768]{0:T(1024)}, u32[]{:S(2)}) copy-start(f32[768]{0:T(1024)} %param.34) | copy-start | bytes 9220
  176.5 11.1 %copy-start.29 = (bf16[512,768]{1,0:T(8,128)(2,1)}, bf16[512,768]{1,0:T(8,128)(2,1)S(1)}, u32[]{:S(2)}) copy-start(bf16[512,768]{1,0:T(8,128)(2,1)S(1)} %fusion.26) | copy-start | bytes 2359300
  183.4 5.2 copy-start.59
  187.6 7.3 %copy-start.5 = (bf16[4,192,768]{2,1,0:T(8,128)(2,1)}, bf16[4,192,768]{2,1,0:T(8,128)(2,1)S(1)}, u32[]{:S(2)}) copy-start(bf16[4,192,768]{2,1,0:T(8,128)(2,1)S(1)} %get-tuple-element.81) | copy-start | bytes 3538948
  191.7 10.1 %copy-start.8 = (bf16[512,768]{0,1:T(8,128)(2,1)}, bf16[512,768]{0,1:T(8,128)(2,1)S(1)}, u32[]{:S(2)}) copy-start(bf16[512,768]{0,1:T(8,128)(2,1)S(1)} %copy.89) | copy-start | bytes 2359300
  197.1 4.7 copy-start.32
  201.8 7.6 %copy-start.2 = (bf16[512,768]{0,1:T(8,128)(2,1)}, bf16[512,768]{0,1:T(8,128)(2,1)S(1)}, u32[]{:S(2)}) copy-start(bf16[512,768]{0,1:T(8,128)(2,1)S(1)} %copy.90) | copy-start | bytes 2359300
  209.4 6.2 %copy-start.34 = (f32[12,512]{1,0:T(8,128)}, f32[12,512]{1,0:T(8,128)S(1)}, u32[]{:S(2)}) copy-start(f32[12,512]{1,0:T(8,128)S(1)} %get-tuple-element.118) | copy-start | bytes 73732
  209.4 6.2 %copy-start.19 = (bf16[4,192,768]{2,1,0:T(8,128)(2,1)S(1)}, bf16[4,192,768]{2,1,0:T(8,128)(2,1)}, u32[]{:S(2)}) copy-start(bf16[4,192,768]{2,1,0:T(8,128)(2,1)} %get-tuple-element.78) | copy-start | bytes 3538948
  209.4 6.2 %copy-start.56 = (f32[768]{0:T(1024)S(1)}, f32[768]{0:T(1024)}, u32[]{:S(2)}) copy-start(f32[768]{0:T(1024)} %param.41) | copy-start | bytes 9220
  215.7 21.6 %slice-start.5 = ((s8[4718592]{0:T(1024)(128)(4,1)}), s8[524288]{0:T(1024)(128)(4,1)S(1)}, s32[]{:S(2)}) async-start(s8[4718592]{0:T(1024)(128)(4,1)} %bitcast.164), calls=%async_computation.5 | async-start | bytes 1048576
  216.9 35.4 %copy-start.13 = (f32[512,768]{1,0:T(8,128)}, f32[512,768]{1,0:T(8,128)S(1)}, u32[]{:S(2)}) copy-start(f32[512,768]{1,0:T(8,128)S(1)} %get-tuple-element.120) | copy-start | bytes 4718596
  217.0 20.2 %slice-start.6 = ((s8[4718592]{0:T(1024)(128)(4,1)}), s8[4194304]{0:T(1024)(128)(4,1)S(1)}, s32[]{:S(2)}) async-start(s8[4718592]{0:T(1024)(128)(4,1)} %bitcast.164), calls=%async_computation.6 | async-start | bytes 8388608
  217.0 20.2 %copy-start.57 = (f32[768]{0:T(1024)S(1)}, f32[768]{0:T(1024)}, u32[]{:S(2)}) copy-start(f32[768]{0:T(1024)} %param.47) | copy-start | bytes 9220
  237.2 3.0 copy-start.60
  237.2 3.0 copy-start.4
  237.3 3.0 copy-start.36
  241.1 11.2 %slice-start.3 = ((s8[4718592]{0:T(1024)(128)(4,1)}), s8[4194304]{0:T(1024)(128)(4,1)S(1)}, s32[]{:S(2)}) async-start(s8[4718592]{0:T(1024)(128)(4,1)} %bitcast.127), calls=%async_computation.3 | async-start | bytes 8388608
  242.9 9.4 %copy-start.15 = (f32[512,768]{1,0:T(8,128)}, f32[512,768]{1,0:T(8,128)S(1)}, u32[]{:S(2)}) copy-start(f32[512,768]{1,0:T(8,128)S(1)} %get-tuple-element.73) | copy-start | bytes 4718596
  242.9 9.4 %slice-start.4 = ((s8[4718592]{0:T(1024)(128)(4,1)}), s8[524288]{0:T(1024)(128)(4,1)S(1)}, s32[]{:S(2)}) async-start(s8[4718592]{0:T(1024)(128)(4,1)} %bitcast.127), calls=%async_computation.4 | async-start | bytes 1048576
  258.4 3.3 copy-start.61
  261.7 4.8 copy-start.20
  284.2 3.0 copy-start.27
  284.2 3.0 copy-start.35
  294.8 3.4 copy-start.16
  298.2 6.8 %copy-start.26 = (bf16[512,768]{0,1:T(8,128)(2,1)S(1)}, bf16[512,768]{0,1:T(8,128)(2,1)}, u32[]{:S(2)}) copy-start(bf16[512,768]{0,1:T(8,128)(2,1)} %copy.88) | copy-start | bytes 2359300
  298.2 6.8 %copy-start.28 = (bf16[512,768]{0,1:T(8,128)(2,1)S(1)}, bf16[512,768]{0,1:T(8,128)(2,1)}, u32[]{:S(2)}) copy-start(bf16[512,768]{0,1:T(8,128)(2,1)} %copy.93) | copy-start | bytes 2359300
  305.0 10.2 %slice-start = ((s8[12582912]{0:T(1024)(128)(4,1)}), s8[4194304]{0:T(1024)(128)(4,1)S(1)}, s32[]{:S(2)}) async-start(s8[12582912]{0:T(1024)(128)(4,1)} %bitcast.119), calls=%async_computation | async-start | bytes 8388608
  305.0 11.4 %slice-start.1 = ((s8[12582912]{0:T(1024)(128)(4,1)}), s8[4194304]{0:T(1024)(128)(4,1)S(1)}, s32[]{:S(2)}) async-start(s8[12582912]{0:T(1024)(128)(4,1)} %bitcast.119), calls=%async_computation.1 | async-start | bytes 8388608
  305.0 12.6 %slice-start.2 = ((s8[12582912]{0:T(1024)(128)(4,1)}), s8[4194304]{0:T(1024)(128)(4,1)S(1)}, s32[]{:S(2)}) async-start(s8[12582912]{0:T(1024)(128)(4,1)} %bitcast.119), calls=%async_computation.2 | async-start | bytes 8388608
  317.7 6.8 %copy-start.9 = (bf16[512,768]{0,1:T(8,128)(2,1)S(1)}, bf16[512,768]{0,1:T(8,128)(2,1)}, u32[]{:S(2)}) copy-start(bf16[512,768]{0,1:T(8,128)(2,1)} %copy-done.8) | copy-start | bytes 2359300
  324.5 2.9 copy-start.3
  335.0 4.4 copy-start.11
  337.3 2.9 copy-start.7
  337.3 2.9 copy-start.21
  595.8 10.3 %copy-start.23 = (bf16[768,768]{1,0:T(8,128)(2,1)S(1)}, bf16[768,768]{1,0:T(8,128)(2,1)}, u32[]{:S(2)}) copy-start(bf16[768,768]{1,0:T(8,128)(2,1)} %get-tuple-element.40) | copy-start | bytes 3538948
  603.3 4.3 copy-start.22
  606.0 3.2 copy-start.1
  (21 other events, 44.3 us)
